TPU v7x, 128 devices: a whole 4x4x4 slice. The times are simulated.
128 devices in a mesh: freq: 32 (over z, y, core), row: 2 (over x_hi), col: 2 (over x_lo).
Axes of the slice: x: 4 (x_hi: 2, x_lo: 2; x = x_hi * 2 + x_lo), y: 4, z: 4, core: 2. Of those that a mesh axis runs over, the one named last changes fastest.
Arguments:
- signals: bfloat16 [2000, 2048, 320], P(None, ('freq', 'row', 'col')), may hold values from -16 to 16
- block_of: int32 [2048], replicated, may hold values from 0 to 1, as said below
- kept_bins: int32 [32], replicated, may hold values from 0 to 127, as said below
Outputs:
- cross_real: bfloat16 [32, 2048, 2048], P('freq', 'row', 'col')
- cross_imag: bfloat16 [32, 2048, 2048], P('freq', 'row', 'col')
Inputs may be any that keep to these rules, and one draw needn't show every extreme that they name: `block_of`: exactly 1024 stations have each of the two values. `kept_bins`: distinct values.
All inputs are finite; a program needn't handle non-finite values.
Results may differ from a plain program's by a relative error of at most 0.0066.
Values may be sent and summed in bfloat16 or wider, within the bound.
No kernel may reach another device: no remote copies, remote signals or barrier semaphores. Data moves between devices by JAX's collectives and lax.ppermute only.
A program may use at most 128 MiB of HBM per device.

v0:
```python
import math

import jax
import jax.numpy as jnp
from jax import lax
from jax.sharding import PartitionSpec as P

STATIONS = 2048
SAMPLES = 2000
FIRST = 40
CAND = 128


def build_table():
    sample_index = jnp.arange(SAMPLES, dtype=jnp.int32)
    bin_index = jnp.arange(CAND, dtype=jnp.int32) + FIRST
    phase_turns = sample_index[:, None] * bin_index[None, :] % SAMPLES
    phase_angle = phase_turns.astype(jnp.float32) * (2.0 * math.pi / SAMPLES)
    return jnp.concatenate([jnp.cos(phase_angle), -jnp.sin(phase_angle)], axis=1).astype(
        jnp.bfloat16
    )


def whiten(signals, kept_bins):
    samples, local_count, windows = signals.shape
    dft_table = build_table()
    flat_signals = signals.reshape(samples, local_count * windows)
    spectra = lax.dot_general(
        dft_table, flat_signals, (((0,), (0,)), ((), ())), preferred_element_type=jnp.float32
    )
    real_part = spectra[:CAND]
    imag_part = spectra[CAND:]
    band_power = jnp.mean(real_part * real_part + imag_part * imag_part, axis=0)
    whiten_scale = 1.0 / jnp.sqrt(band_power + 1e-06)
    kept_count = kept_bins.shape[0]
    bin_pick = (kept_bins[:, None] == jnp.arange(CAND, dtype=jnp.int32)[None, :]).astype(
        jnp.float32
    )
    stacked = spectra.reshape(2, CAND, local_count * windows)
    picked = jnp.einsum(
        "bk,rkn->rbn",
        bin_pick,
        stacked,
        precision=lax.Precision.HIGHEST,
        preferred_element_type=jnp.float32,
    )
    kept_real = picked[0] * whiten_scale
    kept_imag = picked[1] * whiten_scale
    return jnp.concatenate(
        [
            kept_real.reshape(kept_count, local_count, windows),
            kept_imag.reshape(kept_count, local_count, windows),
        ],
        axis=2,
    ).astype(jnp.bfloat16)


def block_selector(block_of, which, strict_lower):
    member = block_of == which
    place = jnp.dot(strict_lower, member.astype(jnp.bfloat16), preferred_element_type=jnp.float32)
    half_count = STATIONS // 2
    target = jnp.arange(half_count, dtype=jnp.int32).astype(jnp.float32)
    hit = (place[None, :] == target[:, None]) & member[None, :]
    return hit.astype(jnp.bfloat16)


def cross_block(row_panel, col_panel, windows):
    twisted = jnp.concatenate([row_panel[:, windows:], -row_panel[:, :windows]], axis=1)
    contract = (((1,), (1,)), ((), ()))
    real_sum = lax.dot_general(row_panel, col_panel, contract, preferred_element_type=jnp.float32)
    imag_sum = lax.dot_general(twisted, col_panel, contract, preferred_element_type=jnp.float32)
    return ((real_sum / windows).astype(jnp.bfloat16), (imag_sum / windows).astype(jnp.bfloat16))


def on_device(signals, block_of, kept_bins):
    windows = signals.shape[2]
    panels = whiten(signals, kept_bins)
    grouped = lax.all_gather(panels, ("row", "col"), axis=1, tiled=True)
    relaid = lax.all_to_all(grouped, "freq", split_axis=0, concat_axis=1, tiled=True)
    spectra_rows = relaid[0]
    station_index = jnp.arange(STATIONS, dtype=jnp.int32)
    strict_lower = (station_index[None, :] < station_index[:, None]).astype(jnp.bfloat16)
    row_select = block_selector(block_of, lax.axis_index("row"), strict_lower)
    col_select = block_selector(block_of, lax.axis_index("col"), strict_lower)
    row_panel = jnp.dot(row_select, spectra_rows, preferred_element_type=jnp.float32).astype(
        jnp.bfloat16
    )
    col_panel = jnp.dot(col_select, spectra_rows, preferred_element_type=jnp.float32).astype(
        jnp.bfloat16
    )
    cross_real, cross_imag = cross_block(row_panel, col_panel, windows)
    return (cross_real[None], cross_imag[None])


def solution(mesh):
    return jax.shard_map(
        on_device,
        mesh=mesh,
        in_specs=(P(None, ("freq", "row", "col"), None), P(), P()),
        out_specs=(P("freq", "row", "col"), P("freq", "row", "col")),
        check_vma=False,
    )
```

profile of v0, /device:TPU:1, one launch (start us, length us, event | category | flops | bytes accessed | tf_op | source)
XLA Modules:
  0.0 130.4 jit_solution(9389363908548679976)
XLA Ops:
  7.2 0.0 all-gather.2.cloned.1.call-start
  7.2 4.4 %cosine_convert_fusion = (bf16[2000,128]{1,0:T(8,128)(2,1)S(1)}, bf16[2000,128]{1,0:T(8,128)(2,1)S(1)}) fusion(s32[128]{0:T(128)S(1)} %iota_add_fusion), kind=kLoop, calls=%fused_computation.37 | loop fusion | flops 3072000 | bytes 1024512 | tf_op jit(solution)/shard_map/convert.2
  11.6 10.1 %fusion.29 = f32[256,5120]{1,0:T(8,128)S(1)} fusion(bf16[2000,5120]{0,1:T(8,128)(2,1)} %bitcast.26, bf16[2000,128]{1,0:T(8,128)(2,1)S(1)} %get-tuple-element.11, bf16[2000,128]{1,0:T(8,128)(2,1)S(1)} %get-tuple-element.10), kind=kOutput, calls=%fused_computation.32 | convolution fusion | flops 5244928000 | bytes 26746880 | tf_op jit(solution)/shard_map/dot_general | solution.py:28
  21.7 0.0 copy-start
  21.7 0.0 copy-start.2
  21.7 0.4 fusion.15
  22.2 1.8 %copy-done = f32[256,5120]{1,0:T(8,128)} copy-done((f32[256,5120]{1,0:T(8,128)}, f32[256,5120]{1,0:T(8,128)S(1)}, u32[]{:S(2)}) %copy-start) | copy-done | bytes 5242904
  24.0 0.1 sqrt.6
  24.1 0.0 copy-done.2
  24.1 4.5 %convolution_bitcast_fusion = f32[2,32,5120]{2,1,0:T(8,128)S(1)} fusion(f32[2,128,5120]{2,1,0:T(8,128)} %bitcast.23, s32[32]{0:T(128)S(1)} %copy-done.2), kind=kOutput, calls=%fused_computation.9 | convolution fusion | flops 503320576 | bytes 6553728 | tf_op jit(solution)/shard_map/bk,rkn->rbn/dot_general | solution.py:40
  28.6 0.1 fusion.42
  28.7 0.2 squeeze.9
  29.0 0.3 squeeze.10
  29.2 0.1 multiply_convert_fusion.3
  29.4 1.1 pad_maximum_fusion
  30.4 0.0 all-gather.2.cloned.1.call-update
  30.5 0.0 copy-start.1
  30.5 38.5 %all-gather.2.cloned.1.call-done = bf16[32,64,640]{2,1,0:T(8,128)(2,1)} async-done(((bf16[32,16,640]{2,1,0:T(8,128)(2,1)}), bf16[32,64,640]{2,1,0:T(8,128)(2,1)}) %all-gather.2.cloned.1.call-update) | async-done | bytes 2621456 | tf_op jit(solution)/shard_map/all_gather | solution.py:78
  69.0 7.7 %all-to-all-start = ((bf16[32,64,640]{2,1,0:T(8,128)(2,1)}), bf16[32,64,640]{2,1,0:T(8,128)(2,1)S(1)}, u32[]{:S(2)}, u32[]{:S(2)}) async-start(bf16[32,64,640]{2,1,0:T(8,128)(2,1)} %all-gather.2.cloned.1.call-done), calls=%async_computation | async-start | bytes 5242880 | tf_op jit(solution)/shard_map/all_to_all | solution.py:79
  76.7 0.0 copy-done.1
  76.8 1.4 %fusion = f32[1,2048]{1,0:T(1,128)S(1)} fusion(pred[2048,1]{0,1:T(4,128)(4,1)S(1)} %reshape.57), kind=kOutput, calls=%fused_computation.1 | convolution fusion | flops 12582912 | bytes 10240 | tf_op jit(solution)/shard_map/dot_general | solution.py:60
  78.2 1.4 %fusion.1 = f32[1,2048]{1,0:T(1,128)S(1)} fusion(pred[2048,1]{0,1:T(4,128)(4,1)S(1)} %reshape.54), kind=kOutput, calls=%fused_computation.2 | convolution fusion | flops 12582912 | bytes 10240 | tf_op jit(solution)/shard_map/dot_general | solution.py:60
  79.6 30.7 %all-to-all-done = bf16[32,64,640]{2,1,0:T(8,128)(2,1)S(1)} async-done(((bf16[32,64,640]{2,1,0:T(8,128)(2,1)}), bf16[32,64,640]{2,1,0:T(8,128)(2,1)S(1)}, u32[]{:S(2)}, u32[]{:S(2)}) %all-to-all-start) | async-done | bytes 2621472 | tf_op jit(solution)/shard_map/all_to_all | solution.py:79
  110.2 3.7 %fusion.21 = bf16[1024,640]{1,0:T(8,128)(2,1)S(1)} fusion(bf16[2048,640]{1,0:T(8,128)(2,1)S(1)} %bitcast.24, f32[2048]{0:T(1024)S(1)} %bitcast.28, f32[1024]{0:T(1024)S(1)} %iota_convert_fusion, pred[2048]{0:T(1024)(128)(4,1)S(1)} %get-tuple-element.8), kind=kOutput, calls=%fused_computation.25 | convolution fusion | flops 2689204224 | bytes 3946496 | tf_op jit(solution)/shard_map/dot_general | solution.py:88
  114.0 3.1 %fusion.18 = bf16[1024,640]{0,1:T(8,128)(2,1)S(1)} fusion(bf16[2048,640]{1,0:T(8,128)(2,1)S(1)} %bitcast.25, f32[2048]{0:T(1024)S(1)} %bitcast.27, f32[1024]{0:T(1024)S(1)} %iota_convert_fusion, pred[2048]{0:T(1024)(128)(4,1)S(1)} %get-tuple-element.9), kind=kOutput, calls=%fused_computation.24 | convolution fusion | flops 2689204224 | bytes 3946496 | tf_op jit(solution)/shard_map/dot_general | solution.py:85
  117.1 0.1 fusion.41
  117.2 3.2 %fusion.16 = bf16[1,1024,1024]{2,1,0:T(8,128)(2,1)} fusion(bf16[1024,640]{0,1:T(8,128)(2,1)S(1)} %fusion.18, bf16[1024,640]{1,0:T(8,128)(2,1)S(1)} %fusion.21), kind=kOutput, calls=%fused_computation.22 | convolution fusion | flops 1344274432 | bytes 4718592 | tf_op jit(solution)/shard_map/dot_general | solution.py:70
  120.4 3.2 %fusion.17 = bf16[1,1024,1024]{2,1,0:T(8,128)(2,1)} fusion(bf16[1024,640]{1,0:T(8,128)(2,1)S(1)} %fusion.21, bf16[1024,320]{0,1:T(8,128)(2,1)S(1)} %get-tuple-element.3, bf16[1024,320]{0,1:T(8,128)(2,1)S(1)} %get-tuple-element.2), kind=kOutput, calls=%fused_computation.23 | convolution fusion | flops 1346895872 | bytes 4718592 | tf_op jit(solution)/shard_map/dot_general | solution.py:71
  (6 shorter events, 0.0 us)
Async XLA Ops:
  7.2 61.8 %all-gather.2.cloned.1.call-start = ((), (), s32[]{:S(2)}) async-start(), calls=%async_computation.1 | async-start | bytes 3276800 | tf_op jit(solution)/shard_map/all_gather | solution.py:78
  21.7 2.3 %copy-start = (f32[256,5120]{1,0:T(8,128)}, f32[256,5120]{1,0:T(8,128)S(1)}, u32[]{:S(2)}) copy-start(f32[256,5120]{1,0:T(8,128)S(1)} %fusion.29) | copy-start | bytes 15728644
  21.7 2.4 %copy-start.2 = (s32[32]{0:T(128)S(1)}, s32[32]{0:T(128)}, u32[]{:S(2)}) copy-start(s32[32]{0:T(128)} %param.5) | copy-start | bytes 388
  30.5 46.2 %copy-start.1 = (s32[2048]{0:T(1024)S(1)}, s32[2048]{0:T(1024)}, u32[]{:S(2)}) copy-start(s32[2048]{0:T(1024)} %param.4) | copy-start | bytes 24580
  69.0 41.3 %all-to-all-start = ((bf16[32,64,640]{2,1,0:T(8,128)(2,1)}), bf16[32,64,640]{2,1,0:T(8,128)(2,1)S(1)}, u32[]{:S(2)}, u32[]{:S(2)}) async-start(bf16[32,64,640]{2,1,0:T(8,128)(2,1)} %all-gather.2.cloned.1.call-done), calls=%async_computation | async-start | bytes 5242880 | tf_op jit(solution)/shard_map/all_to_all | solution.py:79
Sparse Core Ops, SparseCore 0:
  30.6 38.3 all-gather.1
where the time goes:
time: 132 us; the launch traced here: 130 us
  waiting for transfers between devices  69.2 us (52%)
  matrix products  30.6 us (23%)
  between operations  14.2 us (11%)
  starting transfers between devices  7.75 us (6%)
  other arithmetic  6.12 us (5%)
  local copies, waits for them, and re-layouts  2.54 us (2%)
    all_gather x1, waiting for transfers between devices, on_device(): grouped = lax.all_gather(panels, ('row', 'col'), axis=1, tiled=True)  38.5 us
    all_to_all x1, waiting for transfers between devices, on_device(): lax.all_to_all(grouped, 'freq', split_axis=0, concat_axis=1, tiled=True)  30.7 us
    dot_general x1, matrix products, whiten(): lax.dot_general(dft_table, flat_signals, (((0,), (0,)), ((), ())), prefer...  10.1 us
    all_to_all x1, starting transfers between devices, on_device(): lax.all_to_all(grouped, 'freq', split_axis=0, concat_axis=1, tiled=True)  7.71 us
    dot_general x1, matrix products, whiten(): jnp.einsum('bk,rkn->rbn', bin_pick, stacked, precision=lax.Precision.HIGH...  4.51 us
    another operation x2, other arithmetic  4.51 us
    dot_general x1, matrix products, on_device(): jnp.dot(col_select, spectra_rows, preferred_element_type=jnp.float32)  3.75 us
    dot_general x1, matrix products, cross_block(): lax.dot_general(twisted, col_panel, contract, preferred_element_type=jnp....  3.18 us
  transfers between devices with their start and end apart: 2, of which 2 were waited for; matrix products, arithmetic and copies ran while one was open for 2% of the time, Pallas kernels for 0%

commit v1 on v0

v1 whole, which is shorter than its diff:
```python
import math

import jax
import jax.numpy as jnp
import numpy as np
from jax import lax
from jax.experimental import pallas as pl
from jax.experimental.pallas import tpu as pltpu
from jax.sharding import PartitionSpec as P

STATIONS = 2048
SAMPLES = 2000
FIRST = 40
CAND = 128
WINDOWS = 320
KEPT = 32
LOCAL = 16
WIDE = 2 * WINDOWS
COPIES = 4
HALF = STATIONS // 2
GROUP = 256
GROUPS = STATIONS // GROUP
WINDOW = GROUP + 16
STEP_STATIONS = 2
ROW_TILE = 256
LANES = 128
NT = (((1,), (1,)), ((), ()))


def build_table():
    turns = np.arange(SAMPLES)[:, None] * (np.arange(CAND) + FIRST)[None, :] % SAMPLES
    angle = turns.astype(np.float32) * np.float32(2.0 * math.pi / SAMPLES)
    return np.concatenate([np.cos(angle), -np.sin(angle)], axis=1).astype(jnp.bfloat16)


def whiten_kernel(kept_ref, table_ref, signals_ref, out_ref, pick, rows):
    step = pl.program_id(0)

    @pl.when(step == 0)
    def _():
        lane = lax.broadcasted_iota(jnp.int32, (1, 2 * CAND), 1)
        for b in range(KEPT):
            bin_index = kept_ref[b]
            pick[pl.ds(b, 1), :] = (lane == bin_index).astype(jnp.float32)
            pick[pl.ds(KEPT + b, 1), :] = (lane == CAND + bin_index).astype(jnp.float32)

    flat = signals_ref[...].reshape(STEP_STATIONS * WINDOWS, SAMPLES)
    spectra = jnp.dot(flat, table_ref[...], preferred_element_type=jnp.float32)
    band_power = jnp.sum(spectra * spectra, axis=1, keepdims=True) * (1.0 / CAND)
    whitened = (spectra * lax.rsqrt(band_power + 1e-06)).astype(jnp.bfloat16)
    picked = lax.dot_general(
        pick[...].astype(jnp.bfloat16), whitened, NT, preferred_element_type=jnp.float32
    )
    for j in range(STEP_STATIONS):
        mine = picked[:, j * WINDOWS : (j + 1) * WINDOWS]
        both = jnp.concatenate([mine[:KEPT], mine[KEPT:]], axis=1)
        place = pl.Slice(step * STEP_STATIONS + j, KEPT, LOCAL)
        for t in range(WIDE // LANES):
            rows[t, place, :] = both[:, t * LANES : (t + 1) * LANES]

    @pl.when(step == pl.num_programs(0) - 1)
    def _():
        for t in range(WIDE // LANES):
            panels = rows[t].reshape(KEPT, LOCAL, LANES).astype(jnp.bfloat16)
            for j in range(COPIES):
                out_ref[:, j, :, t * LANES : (t + 1) * LANES] = panels


def whiten(signals, kept_bins):
    return pl.pallas_call(
        whiten_kernel,
        grid=(LOCAL // STEP_STATIONS,),
        in_specs=[
            pl.BlockSpec(memory_space=pltpu.SMEM),
            pl.BlockSpec((SAMPLES, 2 * CAND), lambda i: (0, 0)),
            pl.BlockSpec((STEP_STATIONS, WINDOWS, SAMPLES), lambda i: (i, 0, 0)),
        ],
        out_specs=pl.BlockSpec((KEPT, COPIES, LOCAL, WIDE), lambda i: (0, 0, 0, 0)),
        out_shape=jax.ShapeDtypeStruct((KEPT, COPIES, LOCAL, WIDE), jnp.bfloat16),
        scratch_shapes=[
            pltpu.VMEM((2 * KEPT, 2 * CAND), jnp.float32),
            pltpu.VMEM((WIDE // LANES, KEPT * LOCAL, LANES), jnp.float32),
        ],
        compiler_params=pltpu.CompilerParams(vmem_limit_bytes=48 * 1024 * 1024),
        name="whiten",
    )(kept_bins, build_table(), jnp.transpose(signals, (1, 2, 0)))


def places(block_of, which):
    member = (block_of == which).reshape(GROUPS, GROUP)
    index = np.arange(GROUP)
    before = jnp.asarray((index[:, None] < index[None, :]).astype(jnp.bfloat16))
    ones = member.astype(jnp.bfloat16)
    rank = jnp.dot(ones, before, preferred_element_type=jnp.float32).astype(jnp.int32)
    count = jnp.sum(member.astype(jnp.int32), axis=1)
    group = np.arange(GROUPS)
    earlier = jnp.asarray((group[:, None] < group[None, :]).astype(np.int32))
    offset = jnp.sum(count[:, None] * earlier, axis=0)
    shift = offset % 16
    target = jnp.where(member, rank + shift[:, None], -1)
    return target, offset - shift


def cross_kernel(base_ref, target_ref, panel_ref, real_ref, imag_ref, sorted_rows, sorted_cols):
    step = pl.program_id(0)

    @pl.when(step == 0)
    def _():
        place = lax.broadcasted_iota(jnp.int32, (WINDOW, GROUP), 0)
        for side, dest in ((0, sorted_rows), (1, sorted_cols)):
            dest[0:16, :] = jnp.zeros((16, WIDE), jnp.bfloat16)
            for g in range(GROUPS):
                hit = (place == target_ref[side, g : g + 1, :]).astype(jnp.bfloat16)
                moved = jnp.dot(
                    hit, panel_ref[g * GROUP : (g + 1) * GROUP, :], preferred_element_type=jnp.float32
                ).astype(jnp.bfloat16)
                base = pl.multiple_of(base_ref[side, g], 16)
                dest[pl.ds(base, 16), :] += moved[:16]
                dest[pl.ds(pl.multiple_of(base + 16, 16), GROUP), :] = moved[16:]

    rows = sorted_rows[pl.ds(pl.multiple_of(step * ROW_TILE, ROW_TILE), ROW_TILE), :]
    twisted = jnp.concatenate([rows[:, WINDOWS:], -rows[:, :WINDOWS]], axis=1)
    cols = sorted_cols[0:HALF, :]
    scale = 1.0 / WINDOWS
    real_sum = lax.dot_general(rows, cols, NT, preferred_element_type=jnp.float32)
    real_ref[0] = (real_sum * scale).astype(jnp.bfloat16)
    imag_sum = lax.dot_general(twisted, cols, NT, preferred_element_type=jnp.float32)
    imag_ref[0] = (imag_sum * scale).astype(jnp.bfloat16)


def cross(base, target, panel):
    block = pl.BlockSpec((1, ROW_TILE, HALF), lambda i: (0, i, 0))
    shape = jax.ShapeDtypeStruct((1, HALF, HALF), jnp.bfloat16)
    return pl.pallas_call(
        cross_kernel,
        grid=(HALF // ROW_TILE,),
        in_specs=[
            pl.BlockSpec(memory_space=pltpu.SMEM),
            pl.BlockSpec((2, GROUPS, GROUP), lambda i: (0, 0, 0)),
            pl.BlockSpec((STATIONS, WIDE), lambda i: (0, 0)),
        ],
        out_specs=[block, block],
        out_shape=[shape, shape],
        scratch_shapes=[
            pltpu.VMEM((HALF + WINDOW, WIDE), jnp.bfloat16),
            pltpu.VMEM((HALF + WINDOW, WIDE), jnp.bfloat16),
        ],
        compiler_params=pltpu.CompilerParams(vmem_limit_bytes=48 * 1024 * 1024),
        name="cross",
    )(base, target, panel)


def on_device(signals, block_of, kept_bins):
    panels = whiten(signals, kept_bins).reshape(KEPT * COPIES, LOCAL, WIDE)
    relaid = lax.all_to_all(
        panels, ("freq", "row", "col"), split_axis=0, concat_axis=0, tiled=True
    )
    row_target, row_base = places(block_of, lax.axis_index("row"))
    col_target, col_base = places(block_of, lax.axis_index("col"))
    base = jnp.stack([row_base, col_base])
    target = jnp.stack([row_target, col_target])
    cross_real, cross_imag = cross(base, target, relaid.reshape(STATIONS, WIDE))
    return (cross_real, cross_imag)


def solution(mesh):
    return jax.shard_map(
        on_device,
        mesh=mesh,
        in_specs=(P(None, ("freq", "row", "col"), None), P(), P()),
        out_specs=(P("freq", "row", "col"), P("freq", "row", "col")),
        check_vma=False,
    )
```

time: 132 us -> 73.9 us (0.56)
  waiting for transfers between devices: 69.2 us -> 35.7 us
  matrix products: 30.6 us -> 0.26 us
  Pallas kernels: 0 us -> 23.1 us
  between operations: 14.2 us -> 0.72 us
  other arithmetic: 6.12 us -> 0.36 us
  starting transfers between devices: 7.75 us -> 11.5 us
    all_gather x1 -> x0, waiting for transfers between devices: 38.5 us -> none  [on_device(): grouped = lax.all_gather(panels, ('row', 'col'), axis=1, tiled=True)]
    dot_general x8 -> x2, matrix products: 30.6 us -> 0.26 us  [places(): jnp.dot(ones, before, preferred_element_type=jnp.float32).astype(jnp.int32)]
    pallas_call x0 -> x2, Pallas kernels: none -> 23.1 us  [the longest x1 15.4 us: whiten(): pl.pallas_call(whiten_kernel, grid=(LOCAL // STEP_STATIONS,), in_specs=[p...]
    all_to_all x1, waiting for transfers between devices: 30.7 us -> 35.7 us  [on_device(): lax.all_to_all(panels, ('freq', 'row', 'col'), split_axis=0, concat_axis=...]
    another operation x2, other arithmetic: 4.51 us -> 0.02 us  [the longest x1 0.01 us: on_device(): base = jnp.stack([row_base, col_base])]
    all_to_all x1, starting transfers between devices: 7.71 us -> 11.5 us  [on_device(): lax.all_to_all(panels, ('freq', 'row', 'col'), split_axis=0, concat_axis=...]
  transfers between devices with their start and end apart: 2 -> 1, of which waited for: 2 -> 1; matrix products, arithmetic and copies ran while one was open for 2% -> 1% of each run, Pallas kernels for 0% -> 0%
where the time goes in v1:
time: 73.9 us; the launch traced here: 73.5 us
  waiting for transfers between devices  35.7 us (48%)
  Pallas kernels  23.1 us (31%)
  starting transfers between devices  11.5 us (16%)
  local copies, waits for them, and re-layouts  1.9 us (3%)
    all_to_all x1, waiting for transfers between devices, on_device(): lax.all_to_all(panels, ('freq', 'row', 'col'), split_axis=0, concat_axis=...  35.7 us
    pallas_call x1, Pallas kernels, whiten(): pl.pallas_call(whiten_kernel, grid=(LOCAL // STEP_STATIONS,), in_specs=[p...  15.4 us
    all_to_all x1, starting transfers between devices, on_device(): lax.all_to_all(panels, ('freq', 'row', 'col'), split_axis=0, concat_axis=...  11.5 us
    pallas_call x1, Pallas kernels, cross(): pl.pallas_call(cross_kernel, grid=(HALF // ROW_TILE,), in_specs=[pl.Block...  7.71 us
    unnamed x10, local copies, waits for them, and re-layouts  1.88 us
  transfers between devices with their start and end apart: 1, of which 1 were waited for; matrix products, arithmetic and copies ran while one was open for 1% of the time, Pallas kernels for 0%

profile of v1, /device:TPU:1, one launch (start us, length us, event | category | flops | bytes accessed | tf_op | source)
XLA Modules:
  0.0 73.5 jit_solution(17595632677746437844)
XLA Ops:
  0.6 0.0 copy-start
  0.6 1.2 %copy-done = bf16[2000,256]{1,0:T(8,128)(2,1)S(1)} copy-done((bf16[2000,256]{1,0:T(8,128)(2,1)S(1)}, bf16[2000,256]{1,0:T(8,128)(2,1)}, u32[]{:S(2)}) %copy-start) | copy-done | bytes 1024024
  1.8 0.0 copy-start.1
  1.9 0.7 copy-done.1
  2.5 15.4 %whiten.1 = bf16[32,4,16,640]{3,2,1,0:T(8,128)(2,1)} custom-call(s32[32]{0:T(128)S(1)} %copy-done.1, bf16[2000,256]{1,0:T(8,128)(2,1)S(1)} %copy-done, bf16[16,320,2000]{2,1,0:T(8,128)(2,1)} %bitcast.16), custom_call_target="tpu_custom_call" | custom-call | tf_op jit(solution)/shard_map/whiten/pallas_call | solution.py:70
  17.9 0.0 copy-start.2
  17.9 0.0 copy-start.3
  17.9 0.0 copy-start.4
  17.9 11.5 %all-to-all-start = ((bf16[128,16,640]{2,1,0:T(8,128)(2,1)}), bf16[128,16,640]{2,1,0:T(8,128)(2,1)S(1)}, u32[]{:S(2)}, u32[]{:S(2)}) async-start(bf16[128,16,640]{2,1,0:T(8,128)(2,1)} %bitcast.5), calls=%async_computation | async-start | bytes 5242880 | tf_op jit(solution)/shard_map/all_to_all | solution.py:155
  29.4 0.0 copy-done.2
  29.5 0.1 convert_reduce_fusion
  29.6 0.1 convert_reduce_fusion.1
  29.7 0.0 copy-done.3
  29.7 0.1 multiply_reduce_fusion.1
  29.8 0.0 copy-done.4
  29.8 0.1 fusion.2
  29.9 0.2 fusion.5
  30.1 35.7 %all-to-all-done = bf16[128,16,640]{2,1,0:T(8,128)(2,1)S(1)} async-done(((bf16[128,16,640]{2,1,0:T(8,128)(2,1)}), bf16[128,16,640]{2,1,0:T(8,128)(2,1)S(1)}, u32[]{:S(2)}, u32[]{:S(2)}) %all-to-all-start) | async-done | bytes 2621472 | tf_op jit(solution)/shard_map/all_to_all | solution.py:155
  65.8 7.7 %cross.1 = (bf16[1,1024,1024]{2,1,0:T(8,128)(2,1)}, bf16[1,1024,1024]{2,1,0:T(8,128)(2,1)}) custom-call(s32[2,8]{1,0:T(2,128)S(1)} %pad_add_fusion.1.base_ref, s32[2,8,256]{2,1,0:T(8,128)S(1)} %pad_add_fusion.target_ref, bf16[2048,640]{1,0:T(8,128)(2,1)S(1)} %bitcast.15), custom_call_target="tpu_custom_call" | custom-call | tf_op jit(solution)/shard_map/cross/pallas_call | solution.py:134
  (7 shorter events, 0.1 us)
Async XLA Ops:
  0.6 1.2 %copy-start = (bf16[2000,256]{1,0:T(8,128)(2,1)S(1)}, bf16[2000,256]{1,0:T(8,128)(2,1)}, u32[]{:S(2)}) copy-start(bf16[2000,256]{1,0:T(8,128)(2,1)} %constant.39.clone.table_ref) | copy-start | bytes 3072004
  1.8 0.7 copy-start.1
  17.9 11.5 %copy-start.2 = (s32[2048]{0:T(1024)S(1)}, s32[2048]{0:T(1024)}, u32[]{:S(2)}) copy-start(s32[2048]{0:T(1024)} %param.9) | copy-start | bytes 24580
  17.9 11.8 %copy-start.3 = (s32[8,8]{1,0:T(8,128)S(1)}, s32[8,8]{1,0:T(8,128)}, u32[]{:S(2)}) copy-start(s32[8,8]{1,0:T(8,128)} %constant.41.clone) | copy-start | bytes 772
  17.9 12.0 %copy-start.4 = (bf16[256,256]{1,0:T(8,128)(2,1)S(1)}, bf16[256,256]{1,0:T(8,128)(2,1)}, u32[]{:S(2)}) copy-start(bf16[256,256]{1,0:T(8,128)(2,1)} %constant.40.clone) | copy-start | bytes 393220
  17.9 48.0 %all-to-all-start = ((bf16[128,16,640]{2,1,0:T(8,128)(2,1)}), bf16[128,16,640]{2,1,0:T(8,128)(2,1)S(1)}, u32[]{:S(2)}, u32[]{:S(2)}) async-start(bf16[128,16,640]{2,1,0:T(8,128)(2,1)} %bitcast.5), calls=%async_computation | async-start | bytes 5242880 | tf_op jit(solution)/shard_map/all_to_all | solution.py:155

commit v2 on v1

v2 whole, which is shorter than its diff:
```python
import math

import jax
import jax.numpy as jnp
import numpy as np
from jax import lax
from jax.experimental import pallas as pl
from jax.experimental.pallas import tpu as pltpu
from jax.sharding import PartitionSpec as P

STATIONS = 2048
SAMPLES = 2000
FIRST = 40
CAND = 128
WINDOWS = 320
KEPT = 32
LOCAL = 16
WIDE = 2 * WINDOWS
COPIES = 4
HALF = STATIONS // 2
GROUP = 256
GROUPS = STATIONS // GROUP
WINDOW = GROUP + 16
STEP_STATIONS = 4
DEPTH = 2
ROW_TILE = 256
LANES = 128
NT = (((1,), (1,)), ((), ()))


def build_table():
    turns = np.arange(SAMPLES)[:, None] * (np.arange(CAND) + FIRST)[None, :] % SAMPLES
    angle = turns.astype(np.float32) * np.float32(2.0 * math.pi / SAMPLES)
    return np.concatenate([np.cos(angle), -np.sin(angle)], axis=1).astype(jnp.bfloat16)


def bin_order(kept, chosen):
    lane = lax.broadcasted_iota(jnp.int32, (1, CAND), 1)
    for b in range(KEPT):
        chosen[pl.ds(b, 1), :] = (lane == kept[b]).astype(jnp.float32)
    first = chosen[...]
    other = 1.0 - jnp.sum(first, axis=0, keepdims=True)
    square = (CAND, CAND)
    before = lax.broadcasted_iota(jnp.int32, square, 0) < lax.broadcasted_iota(jnp.int32, square, 1)
    rank = jnp.dot(
        jnp.broadcast_to(other, (8, CAND)).astype(jnp.bfloat16),
        before.astype(jnp.bfloat16),
        preferred_element_type=jnp.float32,
    )[:1]
    place = jnp.where(other > 0.5, rank, -1.0).astype(jnp.int32)
    rest = lax.broadcasted_iota(jnp.int32, (CAND - KEPT, CAND), 0) == place
    rest = rest.astype(jnp.float32)
    none_first, none_rest = jnp.zeros_like(first), jnp.zeros_like(rest)
    halves = ((first, none_first), (none_first, first), (rest, none_rest), (none_rest, rest))
    order = jnp.concatenate([jnp.concatenate(pair, axis=1) for pair in halves], axis=0)
    return order.astype(jnp.bfloat16)


def whiten_kernel(
    kept_hbm,
    table_hbm,
    signals_hbm,
    out_hbm,
    kept,
    table,
    signals,
    chosen,
    spectra_of_last,
    rows,
    panels,
    small_sems,
    sems,
    out_sems,
):
    steps = LOCAL // STEP_STATIONS

    def fetch(i):
        span = pl.ds(i * STEP_STATIONS, STEP_STATIONS)
        return pltpu.make_async_copy(signals_hbm.at[span], signals.at[span], sems.at[i])

    kept_copy = pltpu.make_async_copy(kept_hbm, kept, small_sems.at[0])
    table_copy = pltpu.make_async_copy(table_hbm, table, small_sems.at[1])
    kept_copy.start()
    table_copy.start()
    for i in range(DEPTH):
        fetch(i).start()
    kept_copy.wait()
    order = bin_order(kept, chosen)
    table_copy.wait()
    table[...] = lax.dot_general(
        table[...], order, NT, preferred_element_type=jnp.float32
    ).astype(jnp.bfloat16)

    def finish(spectra, i):
        band_power = jnp.sum(spectra * spectra, axis=1, keepdims=True) * (1.0 / CAND)
        scale = lax.rsqrt(band_power + 1e-06)
        picked = (spectra[:, :LANES] * scale).astype(jnp.bfloat16).T[: 2 * KEPT]
        picked = picked.astype(jnp.float32)
        for j in range(STEP_STATIONS):
            mine = picked[:, j * WINDOWS : (j + 1) * WINDOWS]
            both = jnp.concatenate([mine[:KEPT], mine[KEPT:]], axis=1)
            place = pl.Slice(i * STEP_STATIONS + j, KEPT, LOCAL)
            for t in range(WIDE // LANES):
                rows[t, place, :] = both[:, t * LANES : (t + 1) * LANES]

    spectra_of_last[...] = jnp.zeros_like(spectra_of_last)

    def body(i, carry):
        fetch(i).wait()

        @pl.when(i + DEPTH < steps)
        def _():
            fetch(i + DEPTH).start()

        finish(spectra_of_last[...], jnp.maximum(i - 1, 0))
        flat = signals[pl.ds(i * STEP_STATIONS, STEP_STATIONS)]
        flat = flat.reshape(STEP_STATIONS * WINDOWS, SAMPLES)
        spectra_of_last[...] = jnp.dot(flat, table[...], preferred_element_type=jnp.float32)
        return carry

    lax.fori_loop(0, steps, body, 0)
    finish(spectra_of_last[...], steps - 1)

    def send(t, j):
        lanes = pl.ds(t * LANES, LANES)
        return pltpu.make_async_copy(
            panels.at[t], out_hbm.at[:, j, :, lanes], out_sems.at[t, j]
        )

    for t in range(WIDE // LANES):
        panels[t] = rows[t].reshape(KEPT, LOCAL, LANES).astype(jnp.bfloat16)
        for j in range(COPIES):
            send(t, j).start()
    for t in range(WIDE // LANES):
        for j in range(COPIES):
            send(t, j).wait()


def whiten(signals, kept_bins):
    hbm = pl.BlockSpec(memory_space=pltpu.HBM)
    return pl.pallas_call(
        whiten_kernel,
        in_specs=[hbm, hbm, hbm],
        out_specs=hbm,
        out_shape=jax.ShapeDtypeStruct((KEPT, COPIES, LOCAL, WIDE), jnp.bfloat16),
        scratch_shapes=[
            pltpu.SMEM((KEPT,), jnp.int32),
            pltpu.VMEM((SAMPLES, 2 * CAND), jnp.bfloat16),
            pltpu.VMEM((LOCAL, WINDOWS, SAMPLES), jnp.bfloat16),
            pltpu.VMEM((KEPT, CAND), jnp.float32),
            pltpu.VMEM((STEP_STATIONS * WINDOWS, 2 * CAND), jnp.float32),
            pltpu.VMEM((WIDE // LANES, KEPT * LOCAL, LANES), jnp.float32),
            pltpu.VMEM((WIDE // LANES, KEPT, LOCAL, LANES), jnp.bfloat16),
            pltpu.SemaphoreType.DMA((2,)),
            pltpu.SemaphoreType.DMA((LOCAL // STEP_STATIONS,)),
            pltpu.SemaphoreType.DMA((WIDE // LANES, COPIES)),
        ],
        compiler_params=pltpu.CompilerParams(vmem_limit_bytes=60 * 1024 * 1024),
        name="whiten",
    )(kept_bins, build_table(), jnp.transpose(signals, (1, 2, 0)))


def places(block_of, which):
    member = (block_of == which).reshape(GROUPS, GROUP)
    index = np.arange(GROUP)
    before = jnp.asarray((index[:, None] < index[None, :]).astype(jnp.bfloat16))
    ones = member.astype(jnp.bfloat16)
    rank = jnp.dot(ones, before, preferred_element_type=jnp.float32).astype(jnp.int32)
    count = jnp.sum(member.astype(jnp.int32), axis=1)
    group = np.arange(GROUPS)
    earlier = jnp.asarray((group[:, None] < group[None, :]).astype(np.int32))
    offset = jnp.sum(count[:, None] * earlier, axis=0)
    shift = offset % 16
    target = jnp.where(member, rank + shift[:, None], -1)
    return target, offset - shift


def cross_kernel(
    base_ref, target_ref, panel_ref, real_hbm, imag_hbm, sorted_rows, sorted_cols, out, sems
):
    place = lax.broadcasted_iota(jnp.int32, (WINDOW, GROUP), 0)
    sides = (sorted_rows, sorted_cols)
    for dest in sides:
        dest[0:16, :] = jnp.zeros((16, WIDE), jnp.bfloat16)
    for g in range(GROUPS):
        group = panel_ref[g * GROUP : (g + 1) * GROUP, :]
        for side, dest in enumerate(sides):
            hit = (place == target_ref[side, g : g + 1, :]).astype(jnp.bfloat16)
            moved = jnp.dot(hit, group, preferred_element_type=jnp.float32).astype(jnp.bfloat16)
            base = pl.multiple_of(base_ref[side, g], 16)
            dest[pl.ds(base, 16), :] += moved[:16]
            dest[pl.ds(pl.multiple_of(base + 16, 16), GROUP), :] = moved[16:]

    cols = sorted_cols[0:HALF, :]
    scale = 1.0 / WINDOWS

    def send(i, part):
        span = pl.ds(i * ROW_TILE, ROW_TILE)
        dest = (real_hbm, imag_hbm)[part].at[0, span]
        return pltpu.make_async_copy(out.at[i, part], dest, sems.at[i, part])

    for i in range(HALF // ROW_TILE):
        rows = sorted_rows[i * ROW_TILE : (i + 1) * ROW_TILE, :]
        twisted = jnp.concatenate([rows[:, WINDOWS:], -rows[:, :WINDOWS]], axis=1)
        for part, left in enumerate((rows, twisted)):
            total = lax.dot_general(left, cols, NT, preferred_element_type=jnp.float32)
            out[i, part] = (total * scale).astype(jnp.bfloat16)
            send(i, part).start()
    for i in range(HALF // ROW_TILE):
        for part in range(2):
            send(i, part).wait()


def cross(base, target, panel):
    shape = jax.ShapeDtypeStruct((1, HALF, HALF), jnp.bfloat16)
    hbm = pl.BlockSpec(memory_space=pltpu.HBM)
    vmem = pl.BlockSpec(memory_space=pltpu.VMEM)
    return pl.pallas_call(
        cross_kernel,
        in_specs=[pl.BlockSpec(memory_space=pltpu.SMEM), vmem, vmem],
        out_specs=[hbm, hbm],
        out_shape=[shape, shape],
        scratch_shapes=[
            pltpu.VMEM((HALF + WINDOW, WIDE), jnp.bfloat16),
            pltpu.VMEM((HALF + WINDOW, WIDE), jnp.bfloat16),
            pltpu.VMEM((HALF // ROW_TILE, 2, ROW_TILE, HALF), jnp.bfloat16),
            pltpu.SemaphoreType.DMA((HALF // ROW_TILE, 2)),
        ],
        compiler_params=pltpu.CompilerParams(vmem_limit_bytes=32 * 1024 * 1024),
        name="cross",
    )(base, target, panel)


def on_device(signals, block_of, kept_bins):
    panels = whiten(signals, kept_bins).reshape(KEPT * COPIES, LOCAL, WIDE)
    relaid = lax.all_to_all(
        panels, ("freq", "row", "col"), split_axis=0, concat_axis=0, tiled=True
    )
    row_target, row_base = places(block_of, lax.axis_index("row"))
    col_target, col_base = places(block_of, lax.axis_index("col"))
    base = jnp.stack([row_base, col_base])
    target = jnp.stack([row_target, col_target])
    cross_real, cross_imag = cross(base, target, relaid.reshape(STATIONS, WIDE))
    return (cross_real, cross_imag)


def solution(mesh):
    return jax.shard_map(
        on_device,
        mesh=mesh,
        in_specs=(P(None, ("freq", "row", "col"), None), P(), P()),
        out_specs=(P("freq", "row", "col"), P("freq", "row", "col")),
        check_vma=False,
    )
```

time: 73.9 us -> 68.1 us (0.922)
  Pallas kernels: 23.1 us -> 19.3 us
  local copies, waits for them, and re-layouts: 1.9 us -> 0.04 us
    pallas_call x2, Pallas kernels: 23.1 us -> 19.3 us  [the longest x1 12.2 us: whiten(): pl.pallas_call(whiten_kernel, in_specs=[hbm, hbm, hbm], out_specs=hbm, ou...]
    unnamed x10 -> x6, local copies, waits for them, and re-layouts: 1.88 us -> 0.02 us
where the time goes in v2:
time: 68.1 us; the launch traced here: 68 us
  waiting for transfers between devices  35.7 us (52%)
  Pallas kernels  19.3 us (28%)
  starting transfers between devices  11.5 us (17%)
  between operations  0.74 us (1%)
    all_to_all x1, waiting for transfers between devices, on_device(): lax.all_to_all(panels, ('freq', 'row', 'col'), split_axis=0, concat_axis=...  35.7 us
    pallas_call x1, Pallas kernels, whiten(): pl.pallas_call(whiten_kernel, in_specs=[hbm, hbm, hbm], out_specs=hbm, ou...  12.2 us
    all_to_all x1, starting transfers between devices, on_device(): lax.all_to_all(panels, ('freq', 'row', 'col'), split_axis=0, concat_axis=...  11.5 us
    pallas_call x1, Pallas kernels, cross(): pl.pallas_call(cross_kernel, in_specs=[pl.BlockSpec(memory_space=pltpu.SM...  7.07 us
  transfers between devices with their start and end apart: 1, of which 1 were waited for; matrix products, arithmetic and copies ran while one was open for 1% of the time, Pallas kernels for 0%

profile of v2, /device:TPU:1, one launch (start us, length us, event | category | flops | bytes accessed | tf_op | source)
XLA Modules:
  0.0 68.0 jit_solution(5459276013957374949)
XLA Ops:
  0.6 12.2 %whiten.1 = bf16[32,4,16,640]{3,2,1,0:T(8,128)(2,1)} custom-call(s32[32]{0:T(128)} %kept_hbm.1, bf16[2000,256]{1,0:T(8,128)(2,1)} %constant.39.clone.table_hbm, bf16[16,320,2000]{2,1,0:T(8,128)(2,1)} %bitcast.16), custom_call_target="tpu_custom_call" | custom-call | tf_op jit(solution)/shard_map/whiten/pallas_call | solution.py:141
  12.9 0.0 copy-start
  12.9 0.0 copy-start.1
  12.9 0.0 copy-start.2
  12.9 11.5 %all-to-all-start = ((bf16[128,16,640]{2,1,0:T(8,128)(2,1)}), bf16[128,16,640]{2,1,0:T(8,128)(2,1)S(1)}, u32[]{:S(2)}, u32[]{:S(2)}) async-start(bf16[128,16,640]{2,1,0:T(8,128)(2,1)} %bitcast.17), calls=%async_computation | async-start | bytes 5242880 | tf_op jit(solution)/shard_map/all_to_all | solution.py:236
  24.4 0.0 copy-done
  24.5 0.1 convert_reduce_fusion
  24.6 0.1 convert_reduce_fusion.1
  24.7 0.0 copy-done.1
  24.7 0.1 multiply_reduce_fusion.1
  24.9 0.0 copy-done.2
  24.9 0.1 fusion.2
  25.0 0.2 fusion.5
  25.1 35.7 %all-to-all-done = bf16[128,16,640]{2,1,0:T(8,128)(2,1)S(1)} async-done(((bf16[128,16,640]{2,1,0:T(8,128)(2,1)}), bf16[128,16,640]{2,1,0:T(8,128)(2,1)S(1)}, u32[]{:S(2)}, u32[]{:S(2)}) %all-to-all-start) | async-done | bytes 2621472 | tf_op jit(solution)/shard_map/all_to_all | solution.py:236
  60.9 7.1 %cross.1 = (bf16[1,1024,1024]{2,1,0:T(8,128)(2,1)}, bf16[1,1024,1024]{2,1,0:T(8,128)(2,1)}) custom-call(s32[2,8]{1,0:T(2,128)S(1)} %pad_add_fusion.1.base_ref, s32[2,8,256]{2,1,0:T(8,128)S(1)} %pad_add_fusion.target_ref, bf16[2048,640]{1,0:T(8,128)(2,1)S(1)} %bitcast.15), custom_call_target="tpu_custom_call" | custom-call | tf_op jit(solution)/shard_map/cross/pallas_call | solution.py:218
  (7 shorter events, 0.1 us)
Async XLA Ops:
  12.9 11.6 %copy-start = (s32[2048]{0:T(1024)S(1)}, s32[2048]{0:T(1024)}, u32[]{:S(2)}) copy-start(s32[2048]{0:T(1024)} %param.9) | copy-start | bytes 24580
  12.9 11.8 %copy-start.1 = (s32[8,8]{1,0:T(8,128)S(1)}, s32[8,8]{1,0:T(8,128)}, u32[]{:S(2)}) copy-start(s32[8,8]{1,0:T(8,128)} %constant.41.clone) | copy-start | bytes 772
  12.9 12.0 %copy-start.2 = (bf16[256,256]{1,0:T(8,128)(2,1)S(1)}, bf16[256,256]{1,0:T(8,128)(2,1)}, u32[]{:S(2)}) copy-start(bf16[256,256]{1,0:T(8,128)(2,1)} %constant.40.clone) | copy-start | bytes 393220
  12.9 48.0 %all-to-all-start = ((bf16[128,16,640]{2,1,0:T(8,128)(2,1)}), bf16[128,16,640]{2,1,0:T(8,128)(2,1)S(1)}, u32[]{:S(2)}, u32[]{:S(2)}) async-start(bf16[128,16,640]{2,1,0:T(8,128)(2,1)} %bitcast.17), calls=%async_computation | async-start | bytes 5242880 | tf_op jit(solution)/shard_map/all_to_all | solution.py:236

commit v3 on v2

--- a/solution.py
+++ b/solution.py
@@ -21,7 +21,9 @@
 GROUP = 256
 GROUPS = STATIONS // GROUP
 WINDOW = GROUP + 16
-STEP_STATIONS = 4
+PAIR = GROUP + 48
+SPAN = 64
+STEPS = WINDOWS // SPAN
 DEPTH = 2
 ROW_TILE = 256
 LANES = 128
@@ -72,11 +74,15 @@
     sems,
     out_sems,
 ):
-    steps = LOCAL // STEP_STATIONS
-
     def fetch(i):
-        span = pl.ds(i * STEP_STATIONS, STEP_STATIONS)
-        return pltpu.make_async_copy(signals_hbm.at[span], signals.at[span], sems.at[i])
+        span = pl.ds(pl.multiple_of(i * SPAN, SPAN), SPAN)
+        return pltpu.make_async_copy(signals_hbm.at[:, span], signals.at[i], sems.at[i])
+
+    def send(i, j):
+        lanes = pl.ds(pl.multiple_of(i * LANES, LANES), LANES)
+        return pltpu.make_async_copy(
+            panels.at[i], out_hbm.at[:, j, :, lanes], out_sems.at[i, j]
+        )
 
     kept_copy = pltpu.make_async_copy(kept_hbm, kept, small_sems.at[0])
     table_copy = pltpu.make_async_copy(table_hbm, table, small_sems.at[1])
@@ -90,50 +96,49 @@
     table[...] = lax.dot_general(
         table[...], order, NT, preferred_element_type=jnp.float32
     ).astype(jnp.bfloat16)
+    low = lax.broadcasted_iota(jnp.int32, (KEPT, LANES), 1) < SPAN
 
     def finish(spectra, i):
         band_power = jnp.sum(spectra * spectra, axis=1, keepdims=True) * (1.0 / CAND)
         scale = lax.rsqrt(band_power + 1e-06)
         picked = (spectra[:, :LANES] * scale).astype(jnp.bfloat16).T[: 2 * KEPT]
         picked = picked.astype(jnp.float32)
-        for j in range(STEP_STATIONS):
-            mine = picked[:, j * WINDOWS : (j + 1) * WINDOWS]
-            both = jnp.concatenate([mine[:KEPT], mine[KEPT:]], axis=1)
-            place = pl.Slice(i * STEP_STATIONS + j, KEPT, LOCAL)
-            for t in range(WIDE // LANES):
-                rows[t, place, :] = both[:, t * LANES : (t + 1) * LANES]
+        for pair in range(LOCAL // 2):
+            real = picked[:KEPT, pair * LANES : (pair + 1) * LANES]
+            imag = picked[KEPT:, pair * LANES : (pair + 1) * LANES]
+            even = jnp.where(low, real, pltpu.roll(imag, SPAN, 1))
+            odd = jnp.where(low, pltpu.roll(real, SPAN, 1), imag)
+            rows[pl.Slice(2 * pair, KEPT, LOCAL), :] = even
+            rows[pl.Slice(2 * pair + 1, KEPT, LOCAL), :] = odd
+        panels[i] = rows[...].reshape(KEPT, LOCAL, LANES).astype(jnp.bfloat16)
 
     spectra_of_last[...] = jnp.zeros_like(spectra_of_last)
 
     def body(i, carry):
         fetch(i).wait()
 
-        @pl.when(i + DEPTH < steps)
+        @pl.when(i + DEPTH < STEPS)
         def _():
             fetch(i + DEPTH).start()
 
         finish(spectra_of_last[...], jnp.maximum(i - 1, 0))
-        flat = signals[pl.ds(i * STEP_STATIONS, STEP_STATIONS)]
-        flat = flat.reshape(STEP_STATIONS * WINDOWS, SAMPLES)
+        flat = signals[i].reshape(LOCAL * SPAN, SAMPLES)
         spectra_of_last[...] = jnp.dot(flat, table[...], preferred_element_type=jnp.float32)
+
+        @pl.when(i > 0)
+        def _():
+            for j in range(COPIES):
+                send(i - 1, j).start()
+
         return carry
 
-    lax.fori_loop(0, steps, body, 0)
-    finish(spectra_of_last[...], steps - 1)
-
-    def send(t, j):
-        lanes = pl.ds(t * LANES, LANES)
-        return pltpu.make_async_copy(
-            panels.at[t], out_hbm.at[:, j, :, lanes], out_sems.at[t, j]
-        )
-
-    for t in range(WIDE // LANES):
-        panels[t] = rows[t].reshape(KEPT, LOCAL, LANES).astype(jnp.bfloat16)
+    lax.fori_loop(0, STEPS, body, 0)
+    finish(spectra_of_last[...], STEPS - 1)
+    for j in range(COPIES):
+        send(STEPS - 1, j).start()
+    for i in range(STEPS):
         for j in range(COPIES):
-            send(t, j).start()
-    for t in range(WIDE // LANES):
-        for j in range(COPIES):
-            send(t, j).wait()
+            send(i, j).wait()
 
 
 def whiten(signals, kept_bins):
@@ -146,21 +151,21 @@
         scratch_shapes=[
             pltpu.SMEM((KEPT,), jnp.int32),
             pltpu.VMEM((SAMPLES, 2 * CAND), jnp.bfloat16),
-            pltpu.VMEM((LOCAL, WINDOWS, SAMPLES), jnp.bfloat16),
+            pltpu.VMEM((STEPS, LOCAL, SPAN, SAMPLES), jnp.bfloat16),
             pltpu.VMEM((KEPT, CAND), jnp.float32),
-            pltpu.VMEM((STEP_STATIONS * WINDOWS, 2 * CAND), jnp.float32),
-            pltpu.VMEM((WIDE // LANES, KEPT * LOCAL, LANES), jnp.float32),
-            pltpu.VMEM((WIDE // LANES, KEPT, LOCAL, LANES), jnp.bfloat16),
+            pltpu.VMEM((LOCAL * SPAN, 2 * CAND), jnp.float32),
+            pltpu.VMEM((KEPT * LOCAL, LANES), jnp.float32),
+            pltpu.VMEM((STEPS, KEPT, LOCAL, LANES), jnp.bfloat16),
             pltpu.SemaphoreType.DMA((2,)),
-            pltpu.SemaphoreType.DMA((LOCAL // STEP_STATIONS,)),
-            pltpu.SemaphoreType.DMA((WIDE // LANES, COPIES)),
+            pltpu.SemaphoreType.DMA((STEPS,)),
+            pltpu.SemaphoreType.DMA((STEPS, COPIES)),
         ],
         compiler_params=pltpu.CompilerParams(vmem_limit_bytes=60 * 1024 * 1024),
         name="whiten",
     )(kept_bins, build_table(), jnp.transpose(signals, (1, 2, 0)))
 
 
-def places(block_of, which):
+def ranks(block_of, which):
     member = (block_of == which).reshape(GROUPS, GROUP)
     index = np.arange(GROUP)
     before = jnp.asarray((index[:, None] < index[None, :]).astype(jnp.bfloat16))
@@ -170,26 +175,41 @@
     group = np.arange(GROUPS)
     earlier = jnp.asarray((group[:, None] < group[None, :]).astype(np.int32))
     offset = jnp.sum(count[:, None] * earlier, axis=0)
-    shift = offset % 16
-    target = jnp.where(member, rank + shift[:, None], -1)
-    return target, offset - shift
+    return member, rank, count, offset
+
+
+def places(block_of, row, col):
+    member, rank, count, offset = ranks(block_of, row)
+    col_member, col_rank, _, col_offset = ranks(block_of, col)
+    shift, col_shift = offset % 16, col_offset % 16
+    second = jnp.where(row == col, 0, (shift + count) // 16 * 16 + 16)
+    col_target = jnp.where(col_member, col_rank + (second + col_shift)[:, None], -1)
+    target = jnp.where(member, rank + shift[:, None], col_target)
+    return target, jnp.stack([offset - shift, col_offset - col_shift, second])
 
 
 def cross_kernel(
-    base_ref, target_ref, panel_ref, real_hbm, imag_hbm, sorted_rows, sorted_cols, out, sems
+    base_ref, target_ref, panel_ref, real_hbm, imag_hbm, sorted_rows, sorted_cols, both, out, sems
 ):
-    place = lax.broadcasted_iota(jnp.int32, (WINDOW, GROUP), 0)
+    place = lax.broadcasted_iota(jnp.int32, (PAIR, GROUP), 0)
     sides = (sorted_rows, sorted_cols)
     for dest in sides:
         dest[0:16, :] = jnp.zeros((16, WIDE), jnp.bfloat16)
+    both[:, PAIR:, :] = jnp.zeros((2, WINDOW, WIDE), jnp.bfloat16)
     for g in range(GROUPS):
         group = panel_ref[g * GROUP : (g + 1) * GROUP, :]
+        hit = (place == target_ref[g : g + 1, :]).astype(jnp.bfloat16)
+        slot = g % 2
+        both[slot, 0:PAIR, :] = jnp.dot(hit, group, preferred_element_type=jnp.float32).astype(
+            jnp.bfloat16
+        )
         for side, dest in enumerate(sides):
-            hit = (place == target_ref[side, g : g + 1, :]).astype(jnp.bfloat16)
-            moved = jnp.dot(hit, group, preferred_element_type=jnp.float32).astype(jnp.bfloat16)
+            start = pl.multiple_of(base_ref[2, g], 16) if side else 0
             base = pl.multiple_of(base_ref[side, g], 16)
-            dest[pl.ds(base, 16), :] += moved[:16]
-            dest[pl.ds(pl.multiple_of(base + 16, 16), GROUP), :] = moved[16:]
+            dest[pl.ds(base, 16), :] += both[slot, pl.ds(start, 16), :]
+            dest[pl.ds(pl.multiple_of(base + 16, 16), GROUP), :] = both[
+                slot, pl.ds(pl.multiple_of(start + 16, 16), GROUP), :
+            ]
 
     cols = sorted_cols[0:HALF, :]
     scale = 1.0 / WINDOWS
@@ -201,7 +221,9 @@
 
     for i in range(HALF // ROW_TILE):
         rows = sorted_rows[i * ROW_TILE : (i + 1) * ROW_TILE, :]
-        twisted = jnp.concatenate([rows[:, WINDOWS:], -rows[:, :WINDOWS]], axis=1)
+        halves = [rows[:, k * SPAN : (k + 1) * SPAN] for k in range(2 * STEPS)]
+        turned = [(halves[2 * k + 1], -halves[2 * k]) for k in range(STEPS)]
+        twisted = jnp.concatenate([half for pair in turned for half in pair], axis=1)
         for part, left in enumerate((rows, twisted)):
             total = lax.dot_general(left, cols, NT, preferred_element_type=jnp.float32)
             out[i, part] = (total * scale).astype(jnp.bfloat16)
@@ -223,6 +245,7 @@
         scratch_shapes=[
             pltpu.VMEM((HALF + WINDOW, WIDE), jnp.bfloat16),
             pltpu.VMEM((HALF + WINDOW, WIDE), jnp.bfloat16),
+            pltpu.VMEM((2, PAIR + WINDOW, WIDE), jnp.bfloat16),
             pltpu.VMEM((HALF // ROW_TILE, 2, ROW_TILE, HALF), jnp.bfloat16),
             pltpu.SemaphoreType.DMA((HALF // ROW_TILE, 2)),
         ],
@@ -236,10 +259,7 @@
     relaid = lax.all_to_all(
         panels, ("freq", "row", "col"), split_axis=0, concat_axis=0, tiled=True
     )
-    row_target, row_base = places(block_of, lax.axis_index("row"))
-    col_target, col_base = places(block_of, lax.axis_index("col"))
-    base = jnp.stack([row_base, col_base])
-    target = jnp.stack([row_target, col_target])
+    target, base = places(block_of, lax.axis_index("row"), lax.axis_index("col"))
     cross_real, cross_imag = cross(base, target, relaid.reshape(STATIONS, WIDE))
     return (cross_real, cross_imag)
 

time: 68.1 us -> 66.6 us (0.978)
  Pallas kernels: 19.3 us -> 17.8 us
    pallas_call x1, Pallas kernels: 12.2 us -> 11.3 us  [whiten(): pl.pallas_call(whiten_kernel, in_specs=[hbm, hbm, hbm], out_specs=hbm, ou...]
where the time goes in v3:
time: 66.6 us; the launch traced here: 66.4 us
  waiting for transfers between devices  35.8 us (54%)
  Pallas kernels  17.8 us (27%)
  starting transfers between devices  11.5 us (17%)
  between operations  0.74 us (1%)
    all_to_all x1, waiting for transfers between devices, on_device(): lax.all_to_all(panels, ('freq', 'row', 'col'), split_axis=0, concat_axis=...  35.8 us
    all_to_all x1, starting transfers between devices, on_device(): lax.all_to_all(panels, ('freq', 'row', 'col'), split_axis=0, concat_axis=...  11.5 us
    pallas_call x1, Pallas kernels, whiten(): pl.pallas_call(whiten_kernel, in_specs=[hbm, hbm, hbm], out_specs=hbm, ou...  11.3 us
    pallas_call x1, Pallas kernels, cross(): pl.pallas_call(cross_kernel, in_specs=[pl.BlockSpec(memory_space=pltpu.SM...  6.53 us
  transfers between devices with their start and end apart: 1, of which 1 were waited for; matrix products, arithmetic and copies ran while one was open for 1% of the time, Pallas kernels for 0%

profile of v3, /device:TPU:1, one launch (start us, length us, event | category | flops | bytes accessed | tf_op | source)
XLA Modules:
  0.0 66.4 jit_solution(12369717571112403119)
XLA Ops:
  0.6 11.3 %whiten.1 = bf16[32,4,16,640]{3,2,1,0:T(8,128)(2,1)} custom-call(s32[32]{0:T(128)} %kept_hbm.1, bf16[2000,256]{1,0:T(8,128)(2,1)} %constant.52.clone.table_hbm, bf16[16,320,2000]{2,1,0:T(8,128)(2,1)} %bitcast.21), custom_call_target="tpu_custom_call" | custom-call | tf_op jit(solution)/shard_map/whiten/pallas_call | solution.py:146
  11.9 0.0 copy-start
  11.9 0.0 copy-start.1
  11.9 0.0 copy-start.2
  11.9 11.5 %all-to-all-start = ((bf16[128,16,640]{2,1,0:T(8,128)(2,1)}), bf16[128,16,640]{2,1,0:T(8,128)(2,1)S(1)}, u32[]{:S(2)}, u32[]{:S(2)}) async-start(bf16[128,16,640]{2,1,0:T(8,128)(2,1)} %bitcast.22), calls=%async_computation | async-start | bytes 5242880 | tf_op jit(solution)/shard_map/all_to_all | solution.py:259
  23.5 0.0 copy-done
  23.5 0.1 convert_reduce_fusion
  23.7 0.0 copy-done.1
  23.7 0.1 multiply_reduce_fusion
  23.8 0.0 copy-done.2
  23.8 0.1 fusion.3
  23.9 0.2 fusion.2.target_ref
  24.1 35.8 %all-to-all-done = bf16[128,16,640]{2,1,0:T(8,128)(2,1)S(1)} async-done(((bf16[128,16,640]{2,1,0:T(8,128)(2,1)}), bf16[128,16,640]{2,1,0:T(8,128)(2,1)S(1)}, u32[]{:S(2)}, u32[]{:S(2)}) %all-to-all-start) | async-done | bytes 2621472 | tf_op jit(solution)/shard_map/all_to_all | solution.py:259
  59.9 6.5 %cross.1 = (bf16[1,1024,1024]{2,1,0:T(8,128)(2,1)}, bf16[1,1024,1024]{2,1,0:T(8,128)(2,1)}) custom-call(s32[3,8]{1,0:T(4,128)S(1)} %pad_add_fusion.base_ref, s32[8,256]{1,0:T(8,128)S(1)} %fusion.2.target_ref, bf16[2048,640]{1,0:T(8,128)(2,1)S(1)} %bitcast.20), custom_call_target="tpu_custom_call" | custom-call | tf_op jit(solution)/shard_map/cross/pallas_call | solution.py:240
  (7 shorter events, 0.1 us)
Async XLA Ops:
  11.9 11.6 %copy-start = (s32[2048]{0:T(1024)S(1)}, s32[2048]{0:T(1024)}, u32[]{:S(2)}) copy-start(s32[2048]{0:T(1024)} %param.9) | copy-start | bytes 24580
  11.9 11.8 %copy-start.1 = (s32[8,8]{1,0:T(8,128)S(1)}, s32[8,8]{1,0:T(8,128)}, u32[]{:S(2)}) copy-start(s32[8,8]{1,0:T(8,128)} %constant.54.clone) | copy-start | bytes 772
  11.9 11.9 %copy-start.2 = (bf16[256,256]{1,0:T(8,128)(2,1)S(1)}, bf16[256,256]{1,0:T(8,128)(2,1)}, u32[]{:S(2)}) copy-start(bf16[256,256]{1,0:T(8,128)(2,1)} %constant.53.clone) | copy-start | bytes 393220
  11.9 48.0 %all-to-all-start = ((bf16[128,16,640]{2,1,0:T(8,128)(2,1)}), bf16[128,16,640]{2,1,0:T(8,128)(2,1)S(1)}, u32[]{:S(2)}, u32[]{:S(2)}) async-start(bf16[128,16,640]{2,1,0:T(8,128)(2,1)} %bitcast.22), calls=%async_computation | async-start | bytes 5242880 | tf_op jit(solution)/shard_map/all_to_all | solution.py:259

commit v4 on v3

--- a/solution.py
+++ b/solution.py
@@ -88,11 +88,11 @@
     table_copy = pltpu.make_async_copy(table_hbm, table, small_sems.at[1])
     kept_copy.start()
     table_copy.start()
-    for i in range(DEPTH):
-        fetch(i).start()
+    fetch(0).start()
     kept_copy.wait()
     order = bin_order(kept, chosen)
     table_copy.wait()
+    fetch(1).start()
     table[...] = lax.dot_general(
         table[...], order, NT, preferred_element_type=jnp.float32
     ).astype(jnp.bfloat16)

time: 66.6 us -> 66.2 us (level)
  no operation moved by 1% of the time
where the time goes in v4:
time: 66.2 us; the launch traced here: 66 us
  waiting for transfers between devices  35.8 us (54%)
  Pallas kernels  17.4 us (26%)
  starting transfers between devices  11.5 us (17%)
  between operations  0.74 us (1%)
    all_to_all x1, waiting for transfers between devices, on_device(): lax.all_to_all(panels, ('freq', 'row', 'col'), split_axis=0, concat_axis=...  35.8 us
    all_to_all x1, starting transfers between devices, on_device(): lax.all_to_all(panels, ('freq', 'row', 'col'), split_axis=0, concat_axis=...  11.5 us
    pallas_call x1, Pallas kernels, whiten(): pl.pallas_call(whiten_kernel, in_specs=[hbm, hbm, hbm], out_specs=hbm, ou...  10.9 us
    pallas_call x1, Pallas kernels, cross(): pl.pallas_call(cross_kernel, in_specs=[pl.BlockSpec(memory_space=pltpu.SM...  6.51 us
  transfers between devices with their start and end apart: 1, of which 1 were waited for; matrix products, arithmetic and copies ran while one was open for 1% of the time, Pallas kernels for 0%

profile of v4, /device:TPU:1, one launch (start us, length us, event | category | flops | bytes accessed | tf_op | source)
XLA Modules:
  0.0 66.0 jit_solution(1391755843355758806)
XLA Ops:
  0.6 10.9 %whiten.1 = bf16[32,4,16,640]{3,2,1,0:T(8,128)(2,1)} custom-call(s32[32]{0:T(128)} %kept_hbm.1, bf16[2000,256]{1,0:T(8,128)(2,1)} %constant.52.clone.table_hbm, bf16[16,320,2000]{2,1,0:T(8,128)(2,1)} %bitcast.21), custom_call_target="tpu_custom_call" | custom-call | tf_op jit(solution)/shard_map/whiten/pallas_call | solution.py:146
  11.5 0.0 copy-start
  11.5 0.0 copy-start.1
  11.5 0.0 copy-start.2
  11.6 11.5 %all-to-all-start = ((bf16[128,16,640]{2,1,0:T(8,128)(2,1)}), bf16[128,16,640]{2,1,0:T(8,128)(2,1)S(1)}, u32[]{:S(2)}, u32[]{:S(2)}) async-start(bf16[128,16,640]{2,1,0:T(8,128)(2,1)} %bitcast.22), calls=%async_computation | async-start | bytes 5242880 | tf_op jit(solution)/shard_map/all_to_all | solution.py:259
  23.1 0.0 copy-done
  23.1 0.1 convert_reduce_fusion
  23.3 0.0 copy-done.1
  23.3 0.1 multiply_reduce_fusion
  23.5 0.0 copy-done.2
  23.5 0.1 fusion.3
  23.6 0.2 fusion.2.target_ref
  23.7 35.8 %all-to-all-done = bf16[128,16,640]{2,1,0:T(8,128)(2,1)S(1)} async-done(((bf16[128,16,640]{2,1,0:T(8,128)(2,1)}), bf16[128,16,640]{2,1,0:T(8,128)(2,1)S(1)}, u32[]{:S(2)}, u32[]{:S(2)}) %all-to-all-start) | async-done | bytes 2621472 | tf_op jit(solution)/shard_map/all_to_all | solution.py:259
  59.5 6.5 %cross.1 = (bf16[1,1024,1024]{2,1,0:T(8,128)(2,1)}, bf16[1,1024,1024]{2,1,0:T(8,128)(2,1)}) custom-call(s32[3,8]{1,0:T(4,128)S(1)} %pad_add_fusion.base_ref, s32[8,256]{1,0:T(8,128)S(1)} %fusion.2.target_ref, bf16[2048,640]{1,0:T(8,128)(2,1)S(1)} %bitcast.20), custom_call_target="tpu_custom_call" | custom-call | tf_op jit(solution)/shard_map/cross/pallas_call | solution.py:240
  (7 shorter events, 0.1 us)
Async XLA Ops:
  11.5 11.6 %copy-start = (s32[2048]{0:T(1024)S(1)}, s32[2048]{0:T(1024)}, u32[]{:S(2)}) copy-start(s32[2048]{0:T(1024)} %param.9) | copy-start | bytes 24580
  11.5 11.7 %copy-start.1 = (s32[8,8]{1,0:T(8,128)S(1)}, s32[8,8]{1,0:T(8,128)}, u32[]{:S(2)}) copy-start(s32[8,8]{1,0:T(8,128)} %constant.54.clone) | copy-start | bytes 772
  11.5 11.9 %copy-start.2 = (bf16[256,256]{1,0:T(8,128)(2,1)S(1)}, bf16[256,256]{1,0:T(8,128)(2,1)}, u32[]{:S(2)}) copy-start(bf16[256,256]{1,0:T(8,128)(2,1)} %constant.53.clone) | copy-start | bytes 393220
  11.6 48.0 %all-to-all-start = ((bf16[128,16,640]{2,1,0:T(8,128)(2,1)}), bf16[128,16,640]{2,1,0:T(8,128)(2,1)S(1)}, u32[]{:S(2)}, u32[]{:S(2)}) async-start(bf16[128,16,640]{2,1,0:T(8,128)(2,1)} %bitcast.22), calls=%async_computation | async-start | bytes 5242880 | tf_op jit(solution)/shard_map/all_to_all | solution.py:259

commit v5 on v4

--- a/solution.py
+++ b/solution.py
@@ -25,7 +25,7 @@
 SPAN = 64
 STEPS = WINDOWS // SPAN
 DEPTH = 2
-ROW_TILE = 256
+ROW_TILE = 128
 LANES = 128
 NT = (((1,), (1,)), ((), ()))
 
@@ -224,9 +224,12 @@
         halves = [rows[:, k * SPAN : (k + 1) * SPAN] for k in range(2 * STEPS)]
         turned = [(halves[2 * k + 1], -halves[2 * k]) for k in range(STEPS)]
         twisted = jnp.concatenate([half for pair in turned for half in pair], axis=1)
-        for part, left in enumerate((rows, twisted)):
-            total = lax.dot_general(left, cols, NT, preferred_element_type=jnp.float32)
-            out[i, part] = (total * scale).astype(jnp.bfloat16)
+        total = lax.dot_general(
+            jnp.concatenate([rows, twisted], axis=0), cols, NT, preferred_element_type=jnp.float32
+        )
+        for part in range(2):
+            mine = total[part * ROW_TILE : (part + 1) * ROW_TILE]
+            out[i, part] = (mine * scale).astype(jnp.bfloat16)
             send(i, part).start()
     for i in range(HALF // ROW_TILE):
         for part in range(2):

time: 66.2 us -> 66.3 us (level)
  no operation moved by 1% of the time
where the time goes in v5:
time: 66.3 us; the launch traced here: 66.1 us
  waiting for transfers between devices  35.8 us (54%)
  Pallas kernels  17.5 us (26%)
  starting transfers between devices  11.5 us (17%)
  between operations  0.74 us (1%)
    all_to_all x1, waiting for transfers between devices, on_device(): lax.all_to_all(panels, ('freq', 'row', 'col'), split_axis=0, concat_axis=...  35.8 us
    all_to_all x1, starting transfers between devices, on_device(): lax.all_to_all(panels, ('freq', 'row', 'col'), split_axis=0, concat_axis=...  11.5 us
    pallas_call x1, Pallas kernels, whiten(): pl.pallas_call(whiten_kernel, in_specs=[hbm, hbm, hbm], out_specs=hbm, ou...  10.9 us
    pallas_call x1, Pallas kernels, cross(): pl.pallas_call(cross_kernel, in_specs=[pl.BlockSpec(memory_space=pltpu.SM...  6.6 us
  transfers between devices with their start and end apart: 1, of which 1 were waited for; matrix products, arithmetic and copies ran while one was open for 1% of the time, Pallas kernels for 0%

profile of v5, /device:TPU:1, one launch (start us, length us, event | category | flops | bytes accessed | tf_op | source)
XLA Modules:
  0.0 66.1 jit_solution(2715720633272874599)
XLA Ops:
  0.6 10.9 %whiten.1 = bf16[32,4,16,640]{3,2,1,0:T(8,128)(2,1)} custom-call(s32[32]{0:T(128)} %kept_hbm.1, bf16[2000,256]{1,0:T(8,128)(2,1)} %constant.52.clone.table_hbm, bf16[16,320,2000]{2,1,0:T(8,128)(2,1)} %bitcast.21), custom_call_target="tpu_custom_call" | custom-call | tf_op jit(solution)/shard_map/whiten/pallas_call | solution.py:146
  11.5 0.0 copy-start
  11.5 0.0 copy-start.1
  11.5 0.0 copy-start.2
  11.6 11.5 %all-to-all-start = ((bf16[128,16,640]{2,1,0:T(8,128)(2,1)}), bf16[128,16,640]{2,1,0:T(8,128)(2,1)S(1)}, u32[]{:S(2)}, u32[]{:S(2)}) async-start(bf16[128,16,640]{2,1,0:T(8,128)(2,1)} %bitcast.22), calls=%async_computation | async-start | bytes 5242880 | tf_op jit(solution)/shard_map/all_to_all | solution.py:262
  23.1 0.0 copy-done
  23.1 0.1 convert_reduce_fusion
  23.3 0.0 copy-done.1
  23.3 0.1 multiply_reduce_fusion
  23.5 0.0 copy-done.2
  23.5 0.1 fusion.3
  23.6 0.2 fusion.2.target_ref
  23.7 35.8 %all-to-all-done = bf16[128,16,640]{2,1,0:T(8,128)(2,1)S(1)} async-done(((bf16[128,16,640]{2,1,0:T(8,128)(2,1)}), bf16[128,16,640]{2,1,0:T(8,128)(2,1)S(1)}, u32[]{:S(2)}, u32[]{:S(2)}) %all-to-all-start) | async-done | bytes 2621472 | tf_op jit(solution)/shard_map/all_to_all | solution.py:262
  59.5 6.6 %cross.1 = (bf16[1,1024,1024]{2,1,0:T(8,128)(2,1)}, bf16[1,1024,1024]{2,1,0:T(8,128)(2,1)}) custom-call(s32[3,8]{1,0:T(4,128)S(1)} %pad_add_fusion.base_ref, s32[8,256]{1,0:T(8,128)S(1)} %fusion.2.target_ref, bf16[2048,640]{1,0:T(8,128)(2,1)S(1)} %bitcast.20), custom_call_target="tpu_custom_call" | custom-call | tf_op jit(solution)/shard_map/cross/pallas_call | solution.py:243
  (7 shorter events, 0.1 us)
Async XLA Ops:
  11.5 11.6 %copy-start = (s32[2048]{0:T(1024)S(1)}, s32[2048]{0:T(1024)}, u32[]{:S(2)}) copy-start(s32[2048]{0:T(1024)} %param.9) | copy-start | bytes 24580
  11.5 11.7 %copy-start.1 = (s32[8,8]{1,0:T(8,128)S(1)}, s32[8,8]{1,0:T(8,128)}, u32[]{:S(2)}) copy-start(s32[8,8]{1,0:T(8,128)} %constant.54.clone) | copy-start | bytes 772
  11.5 11.9 %copy-start.2 = (bf16[256,256]{1,0:T(8,128)(2,1)S(1)}, bf16[256,256]{1,0:T(8,128)(2,1)}, u32[]{:S(2)}) copy-start(bf16[256,256]{1,0:T(8,128)(2,1)} %constant.53.clone) | copy-start | bytes 393220
  11.6 48.0 %all-to-all-start = ((bf16[128,16,640]{2,1,0:T(8,128)(2,1)}), bf16[128,16,640]{2,1,0:T(8,128)(2,1)S(1)}, u32[]{:S(2)}, u32[]{:S(2)}) async-start(bf16[128,16,640]{2,1,0:T(8,128)(2,1)} %bitcast.22), calls=%async_computation | async-start | bytes 5242880 | tf_op jit(solution)/shard_map/all_to_all | solution.py:262
